TPU v7x, 512 devices: a whole 4x4x16 slice. The times are simulated.
512 devices in a mesh: ref: 32 (over z, core), qry: 16 (over x, y).
Axes of the slice: x: 4, y: 4, z: 16, core: 2. Of those that a mesh axis runs over, the one named last changes fastest.
Arguments:
- queries: bfloat16 [4096, 1024], P('qry'), may hold values from -1 to 1
- ref_panels: bfloat16 [256, 128, 1024], P('ref', 'qry'), may hold values from -1 to 1
- cand_mask: int32 [32, 256], P('qry', 'ref'), may hold values 0 or 1
- panel_time: int32 [256], replicated, may hold values from 0 to 255, as said below
- w_first: float32 [9, 32], replicated, may hold values from -2 to 2
- b_first: float32 [32], replicated, may hold values from -2.5 to 2.5
- w_second: bfloat16 [9, 32], replicated, may hold values from -0.375 to 0.375
Outputs:
- score_map: bfloat16 [4096, 32768], P('qry', 'ref')
Inputs may be any that keep to these rules, and one draw needn't show every extreme that they name: `panel_time`: A permutation of the reference time blocks. The owner of block t is t // 8; every owner has 8 blocks. The 8 panels of one ingest index of ref (panels held by one index) include at most 1 of one owner, and every ingest index has 1 panel of some owner.
All inputs are finite; a program needn't handle non-finite values. No bound on the sum of `cand_mask` on one device may be relied on, other than what follows from the above.
Results may differ from a plain program's by a relative error of at most 0.0059.
Values may be sent and summed in bfloat16 or wider, within the bound.
No kernel may reach another device: no remote copies, remote signals or barrier semaphores. Data moves between devices by JAX's collectives and lax.ppermute only.
A program may use at most 64 MiB of HBM per device.

v0:
```python
import math
import jax
import jax.numpy as jnp
from jax import lax
from jax.sharding import PartitionSpec as P

FRAMES = 256


def with_halo(cells, sides, width):
    for axis, dim in sides:
        count = lax.axis_size(axis)
        ends = count - 1
        head = lax.slice_in_dim(cells, 0, width, axis=dim)
        tail = lax.slice_in_dim(cells, cells.shape[dim] - width, cells.shape[dim], axis=dim)
        cells = jnp.concatenate(
            [
                lax.ppermute(tail, axis, [(i, (i + 1) % count) for i in range(ends)]),
                cells,
                lax.ppermute(head, axis, [((i + 1) % count, i) for i in range(ends)]),
            ],
            axis=dim,
        )
    return cells


def layer_one(strip_cols, w_first, b_first):
    height = strip_cols.shape[0]
    widths = strip_cols.shape[1] - 2
    padded = jnp.pad(strip_cols.astype(jnp.float32), ((1, 1), (0, 0)))
    summed = jnp.broadcast_to(b_first[:, None, None], (b_first.shape[0], height, widths))
    for row_shift in range(3):
        for col_shift in range(3):
            summed = (
                summed
                + w_first[3 * row_shift + col_shift][:, None, None]
                * padded[row_shift : row_shift + height, col_shift : col_shift + widths][None]
            )
    return jnp.maximum(summed, 0.0).astype(jnp.bfloat16)


def layer_two(hidden, w_second):
    height = hidden.shape[1]
    widths = hidden.shape[2] - 2
    padded = jnp.pad(hidden, ((0, 0), (1, 1), (0, 0)))
    summed = jnp.zeros((height, widths), jnp.float32)
    for row_shift in range(3):
        for col_shift in range(3):
            summed = summed + jnp.einsum(
                "c,chw->hw",
                w_second[3 * row_shift + col_shift],
                padded[:, row_shift : row_shift + height, col_shift : col_shift + widths],
                preferred_element_type=jnp.float32,
            )
    return summed


def shards(queries, ref_panels, cand_mask, panel_time, w_first, b_first, w_second):
    owners_count = lax.axis_size("ref")
    my_owner = lax.axis_index("ref")
    blocks_dev = ref_panels.shape[0]
    frames_dev = queries.shape[0]
    videos = frames_dev // FRAMES
    slot_count = max(1, (2 * blocks_dev + owners_count - 1) // owners_count)
    times = panel_time.reshape(owners_count, blocks_dev)
    owner_ids = times // blocks_dev
    within = times % blocks_dev
    earlier = jnp.arange(blocks_dev)[None, :] < jnp.arange(blocks_dev)[:, None]
    same_owner = owner_ids[:, :, None] == owner_ids[:, None, :]
    ranks = jnp.sum((same_owner & earlier[None]).astype(jnp.int32), axis=2)
    owner_mine = lax.dynamic_index_in_dim(owner_ids, my_owner, 0, keepdims=False)
    rank_mine = lax.dynamic_index_in_dim(ranks, my_owner, 0, keepdims=False)
    dest_ids = jnp.arange(owners_count)
    slot_ids = jnp.arange(slot_count)
    select = (
        (owner_mine[None, None, :] == dest_ids[:, None, None])
        & (rank_mine[None, None, :] == slot_ids[None, :, None])
    ).astype(jnp.bfloat16)
    outgoing = jnp.einsum(
        "oki,ird->okrd", select, ref_panels, preferred_element_type=jnp.float32
    ).astype(jnp.bfloat16)
    incoming = lax.all_to_all(outgoing, "ref", split_axis=0, concat_axis=0, tiled=True)
    placing = (
        (owner_ids == my_owner)[None, :, None, :]
        & (ranks[None, :, None, :] == slot_ids[None, None, :, None])
        & (within[None, :, None, :] == jnp.arange(blocks_dev)[:, None, None, None])
    )
    placement = jnp.sum(placing.astype(jnp.int32), axis=3).astype(jnp.bfloat16)
    owned = jnp.einsum(
        "tsk,skrd->trd", placement, incoming, preferred_element_type=jnp.float32
    ).astype(jnp.bfloat16)
    tiles = jnp.einsum(
        "qd,brd->qbr",
        queries,
        lax.all_gather(owned, "qry", axis=1, tiled=True),
        preferred_element_type=jnp.float32,
    ).astype(jnp.bfloat16)
    panel_len = tiles.shape[2]
    ref_cols = blocks_dev * panel_len
    qblock_count = cand_mask.shape[0]
    keeper = cand_mask.astype(jnp.bfloat16)[:, None, :, None]
    sims = (
        tiles.reshape(qblock_count, frames_dev // qblock_count, blocks_dev, panel_len) * keeper
    ).reshape(videos, FRAMES, ref_cols)
    first_layer = jax.vmap(layer_one, in_axes=(0, None, None))
    second_layer = jax.vmap(layer_two, in_axes=(0, None))
    single = with_halo(sims, (("ref", 2),), 1)
    spread = jnp.pad(single, ((0, 0), (0, 0), (1, 1)))
    first_col = first_layer(spread[:, :, 1:4], w_first, b_first)[:, :, :, 0]
    last_col = first_layer(spread[:, :, ref_cols : ref_cols + 3], w_first, b_first)[:, :, :, 0]
    edge_pair = jnp.stack([first_col, last_col])
    near_cols = with_halo(edge_pair, (("ref", 0),), 1)
    left_fill = near_cols[0]
    right_fill = near_cols[3]
    left_use = my_owner >= 0
    right_use = my_owner >= 0
    block_cols = math.gcd(256, ref_cols)
    count = ref_cols // block_cols

    def one_block(block_index):
        strip_cols = lax.dynamic_slice_in_dim(spread, block_index * block_cols, block_cols + 4, 2)
        hidden = first_layer(strip_cols, w_first, b_first)
        first = jnp.where((block_index == 0) & left_use, left_fill, hidden[:, :, :, 0])
        final = jnp.where((block_index == count - 1) & right_use, right_fill, hidden[:, :, :, -1])
        hidden = hidden.at[:, :, :, 0].set(first).at[:, :, :, -1].set(final)
        return second_layer(hidden, w_second).astype(jnp.bfloat16)

    blocks_out = lax.map(one_block, jnp.arange(count, dtype=jnp.int32))
    return jnp.transpose(blocks_out, (1, 2, 0, 3)).reshape(frames_dev, ref_cols)


def solution(mesh):
    placed = (P("qry", None), P("ref", "qry", None), P("qry", "ref"), P(), P(), P(), P())
    return jax.shard_map(
        shards, mesh=mesh, in_specs=placed, out_specs=P("qry", "ref"), check_vma=False
    )
```

profile of v0, /device:TPU:97, one launch (start us, length us, event | category | flops | bytes accessed | tf_op | source)
XLA Modules:
  0.0 401.1 jit_solution(5966374788965295155)
XLA Ops:
  10.3 14.8 %all-to-all-start = ((bf16[32,1,8,1024]{3,2,1,0:T(8,128)(2,1)}), bf16[32,1,8,1024]{3,2,1,0:T(8,128)(2,1)S(1)}, u32[]{:S(2)}, u32[]{:S(2)}) async-start(bf16[32,1,8,1024]{3,2,1,0:T(8,128)(2,1)} %copy.95), calls=%async_computation | async-start | bytes 1048576 | tf_op jit(solution)/shard_map/all_to_all | solution.py:82
  25.2 30.0 %all-to-all-done = bf16[32,1,8,1024]{3,2,1,0:T(8,128)(2,1)S(1)} async-done(((bf16[32,1,8,1024]{3,2,1,0:T(8,128)(2,1)}), bf16[32,1,8,1024]{3,2,1,0:T(8,128)(2,1)S(1)}, u32[]{:S(2)}, u32[]{:S(2)}) %all-to-all-start) | async-done | bytes 524320 | tf_op jit(solution)/shard_map/all_to_all | solution.py:82
  57.5 53.4 %all-gather.2.cloned.1.call-done = bf16[8,128,1024]{2,0,1:T(8,128)(2,1)} async-done(((bf16[8,8,1024]{2,0,1:T(8,128)(2,1)}), bf16[8,128,1024]{2,0,1:T(8,128)(2,1)}) %all-gather.2.cloned.1.call-update) | async-done | bytes 2097168 | tf_op jit(solution)/shard_map/all_gather | solution.py:95
  110.9 4.0 fusion.52
  115.4 5.8 %collective-permute-start = (bf16[1,256,1]{2,1,0:T(8,128)(2,1)S(1)}, bf16[1,256,1]{2,1,0:T(8,128)(2,1)S(1)}, u32[]{:S(2)}, u32[]{:S(2)}) collective-permute-start(bf16[1,256,1]{2,1,0:T(8,128)(2,1)S(1)} %get-tuple-element.254), channel_id=1, source_target_pairs={{0,16},{16,32},{32,48},{48,64},{64,80},{80,96},{96,112},{112,128},... | collective-permute-start | bytes 1544 | tf_op jit(solution)/shard_map/ppermute | solution.py:18
  123.2 4.8 %collective-permute-done.1 = bf16[1,256,1]{2,1,0:T(8,128)(2,1)S(1)} collective-permute-done((bf16[1,256,1]{2,1,0:T(8,128)(2,1)S(1)}, bf16[1,256,1]{2,1,0:T(8,128)(2,1)S(1)}, u32[]{:S(2)}, u32[]{:S(2)}) %collective-permute-start.1) | collective-permute-done | bytes 544 | tf_op jit(solution)/shard_map/ppermute | solution.py:20
  132.8 4.9 %collective-permute-start.2 = (bf16[1,1,32,256]{3,2,1,0:T(8,128)(2,1)S(1)}, bf16[1,1,32,256]{3,2,1,0:T(8,128)(2,1)}, u32[]{:S(2)}, u32[]{:S(2)}) collective-permute-start(bf16[1,1,32,256]{3,2,1,0:T(8,128)(2,1)S(1)} %maximum_convert_fusion.2), channel_id=1, source_target_pairs={{0,16},{16,32},{32,48},{48,64},{64,80},{80,96},{96,112},{112,128},... | collective-permute-start | bytes 49160 | tf_op jit(solution)/shard_map/ppermute | solution.py:18
  140.0 251.9 %while.15 = (s32[]{:T(128)}, bf16[4,1,256,256]{3,2,1,0:T(8,128)(2,1)}, f32[32]{0:T(128)}, f32[9,32]{1,0:T(8,128)S(1)}, s32[4]{0:T(128)}, /*index=5*/bf16[1,256,1...) while((s32[]{:T(128)}, ...), condition=%wide.region_3.4_spmd, body=%wide.region_2.3_spmd.sunk | while | flops 80692224 | bytes 88695848 | solution.py:128
  149.3 14.2 %maximum_convert_fusion.4 = bf16[1,32,256,258]{2,1,3,0:T(8,128)(2,1)S(1)} fusion(f32[256,258]{0,1:T(8,128)S(1)} %copy.138, f32[32]{0:T(128)S(1)} %get-tuple-element.355, f32[256,258]{0,1:T(8,128)} %copy.139, f32[32]{0:T(128)S(1)} %get-tuple-element.357, f32[256,258]{0,1:T(8,128)} %copy.140, f32[32]{0:T(128)S(1)} %get-tuple-element.359, ...), kind=kLoop, calls=%fused_computation.clone.1 | loop fusion | flops 42270720 | bytes 6606080 | tf_op jit(solution)/shard_map/while/body/eval_jaxpr/vmap()/convert_element_type | solution.py:39
  170.8 3.6 fusion.118
  174.5 3.6 fusion.119
  178.2 3.6 fusion.120
  181.9 2.8 fusion.121
  184.9 2.8 fusion.122
  187.9 2.8 fusion.123
  190.9 3.6 fusion.124
  194.7 3.6 fusion.125
  198.4 3.6 fusion.126
  212.3 14.2 %maximum_convert_fusion.4 = bf16[1,32,256,258]{2,1,3,0:T(8,128)(2,1)S(1)} fusion(f32[256,258]{0,1:T(8,128)S(1)} %copy.138, f32[32]{0:T(128)S(1)} %get-tuple-element.355, f32[256,258]{0,1:T(8,128)} %copy.139, f32[32]{0:T(128)S(1)} %get-tuple-element.357, f32[256,258]{0,1:T(8,128)} %copy.140, f32[32]{0:T(128)S(1)} %get-tuple-element.359, ...), kind=kLoop, calls=%fused_computation.clone.1 | loop fusion | flops 42270720 | bytes 6606080 | tf_op jit(solution)/shard_map/while/body/eval_jaxpr/vmap()/convert_element_type | solution.py:39
  233.8 3.6 fusion.118
  237.5 3.6 fusion.119
  241.2 3.6 fusion.120
  244.9 2.8 fusion.121
  247.9 2.8 fusion.122
  250.9 2.8 fusion.123
  253.9 3.6 fusion.124
  257.7 3.6 fusion.125
  261.4 3.6 fusion.126
  275.2 14.2 %maximum_convert_fusion.4 = bf16[1,32,256,258]{2,1,3,0:T(8,128)(2,1)S(1)} fusion(f32[256,258]{0,1:T(8,128)S(1)} %copy.138, f32[32]{0:T(128)S(1)} %get-tuple-element.355, f32[256,258]{0,1:T(8,128)} %copy.139, f32[32]{0:T(128)S(1)} %get-tuple-element.357, f32[256,258]{0,1:T(8,128)} %copy.140, f32[32]{0:T(128)S(1)} %get-tuple-element.359, ...), kind=kLoop, calls=%fused_computation.clone.1 | loop fusion | flops 42270720 | bytes 6606080 | tf_op jit(solution)/shard_map/while/body/eval_jaxpr/vmap()/convert_element_type | solution.py:39
  296.8 3.6 fusion.118
  300.5 3.6 fusion.119
  304.2 3.6 fusion.120
  307.9 2.8 fusion.121
  310.9 2.8 fusion.122
  313.9 2.8 fusion.123
  316.9 3.6 fusion.124
  320.7 3.6 fusion.125
  324.4 3.6 fusion.126
  338.2 14.2 %maximum_convert_fusion.4 = bf16[1,32,256,258]{2,1,3,0:T(8,128)(2,1)S(1)} fusion(f32[256,258]{0,1:T(8,128)S(1)} %copy.138, f32[32]{0:T(128)S(1)} %get-tuple-element.355, f32[256,258]{0,1:T(8,128)} %copy.139, f32[32]{0:T(128)S(1)} %get-tuple-element.357, f32[256,258]{0,1:T(8,128)} %copy.140, f32[32]{0:T(128)S(1)} %get-tuple-element.359, ...), kind=kLoop, calls=%fused_computation.clone.1 | loop fusion | flops 42270720 | bytes 6606080 | tf_op jit(solution)/shard_map/while/body/eval_jaxpr/vmap()/convert_element_type | solution.py:39
  359.7 3.6 fusion.118
  363.5 3.6 fusion.119
  367.2 3.6 fusion.120
  370.9 2.8 fusion.121
  373.9 2.8 fusion.122
  376.9 2.8 fusion.123
  379.9 3.6 fusion.124
  383.6 3.6 fusion.125
  387.4 3.6 fusion.126
  (160 shorter events, 83.9 us)
Async XLA Ops:
  6.5 104.4 %copy-start = (bf16[256,1024]{1,0:T(8,128)(2,1)S(1)}, bf16[256,1024]{1,0:T(8,128)(2,1)}, u32[]{:S(2)}) copy-start(bf16[256,1024]{1,0:T(8,128)(2,1)} %param.13) | copy-start | bytes 1572868
  10.3 44.8 %all-to-all-start = ((bf16[32,1,8,1024]{3,2,1,0:T(8,128)(2,1)}), bf16[32,1,8,1024]{3,2,1,0:T(8,128)(2,1)S(1)}, u32[]{:S(2)}, u32[]{:S(2)}) async-start(bf16[32,1,8,1024]{3,2,1,0:T(8,128)(2,1)} %copy.95), calls=%async_computation | async-start | bytes 1048576 | tf_op jit(solution)/shard_map/all_to_all | solution.py:82
  25.1 85.8 %all-gather.2.cloned.1.call-start = ((), (), s32[]{:S(2)}) async-start(), calls=%async_computation.1 | async-start | bytes 2228224 | tf_op jit(solution)/shard_map/all_gather | solution.py:95
  57.3 65.9 %copy-start.2 = (f32[9,32]{1,0:T(8,128)S(1)}, f32[9,32]{1,0:T(8,128)}, u32[]{:S(2)}) copy-start(f32[9,32]{1,0:T(8,128)} %param.17) | copy-start | bytes 3460
  115.4 7.7 %collective-permute-start = (bf16[1,256,1]{2,1,0:T(8,128)(2,1)S(1)}, bf16[1,256,1]{2,1,0:T(8,128)(2,1)S(1)}, u32[]{:S(2)}, u32[]{:S(2)}) collective-permute-start(bf16[1,256,1]{2,1,0:T(8,128)(2,1)S(1)} %get-tuple-element.254), channel_id=1, source_target_pairs={{0,16},{16,32},{32,48},{48,64},{64,80},{80,96},{96,112},{112,128},... | collective-permute-start | bytes 1544 | tf_op jit(solution)/shard_map/ppermute | solution.py:18
  121.2 6.8 %collective-permute-start.1 = (bf16[1,256,1]{2,1,0:T(8,128)(2,1)S(1)}, bf16[1,256,1]{2,1,0:T(8,128)(2,1)S(1)}, u32[]{:S(2)}, u32[]{:S(2)}) collective-permute-start(bf16[1,256,1]{2,1,0:T(8,128)(2,1)S(1)} %get-tuple-element.253), channel_id=1, source_target_pairs={{16,0},{32,16},{48,32},{64,48},{80,64},{96,80},{112,96},{128,112},... | collective-permute-start | bytes 1544 | tf_op jit(solution)/shard_map/ppermute | solution.py:20
  130.1 9.3 %collective-permute-start.3 = (bf16[1,1,32,256]{3,2,1,0:T(8,128)(2,1)S(1)}, bf16[1,1,32,256]{3,2,1,0:T(8,128)(2,1)}, u32[]{:S(2)}, u32[]{:S(2)}) collective-permute-start(bf16[1,1,32,256]{3,2,1,0:T(8,128)(2,1)S(1)} %maximum_convert_fusion.1), channel_id=1, source_target_pairs={{16,0},{32,16},{48,32},{64,48},{80,64},{96,80},{112,96},{128,112},... | collective-permute-start | bytes 49160 | tf_op jit(solution)/shard_map/ppermute | solution.py:20
  132.8 6.6 %collective-permute-start.2 = (bf16[1,1,32,256]{3,2,1,0:T(8,128)(2,1)S(1)}, bf16[1,1,32,256]{3,2,1,0:T(8,128)(2,1)}, u32[]{:S(2)}, u32[]{:S(2)}) collective-permute-start(bf16[1,1,32,256]{3,2,1,0:T(8,128)(2,1)S(1)} %maximum_convert_fusion.2), channel_id=1, source_target_pairs={{0,16},{16,32},{32,48},{48,64},{64,80},{80,96},{96,112},{112,128},... | collective-permute-start | bytes 49160 | tf_op jit(solution)/shard_map/ppermute | solution.py:18
  163.5 3.2 copy-start.1
  163.5 7.3 %copy-start.3 = (bf16[9,32]{1,0:T(8,128)(2,1)S(1)}, bf16[9,32]{1,0:T(8,128)(2,1)}, u32[]{:S(2)}) copy-start(bf16[9,32]{1,0:T(8,128)(2,1)} %get-tuple-element.413) | copy-start | bytes 1732 | tf_op jit(solution)/shard_map/while
  226.5 3.2 copy-start.1
  226.5 7.3 %copy-start.3 = (bf16[9,32]{1,0:T(8,128)(2,1)S(1)}, bf16[9,32]{1,0:T(8,128)(2,1)}, u32[]{:S(2)}) copy-start(bf16[9,32]{1,0:T(8,128)(2,1)} %get-tuple-element.413) | copy-start | bytes 1732 | tf_op jit(solution)/shard_map/while
  289.5 3.2 copy-start.1
  289.5 7.3 %copy-start.3 = (bf16[9,32]{1,0:T(8,128)(2,1)S(1)}, bf16[9,32]{1,0:T(8,128)(2,1)}, u32[]{:S(2)}) copy-start(bf16[9,32]{1,0:T(8,128)(2,1)} %get-tuple-element.413) | copy-start | bytes 1732 | tf_op jit(solution)/shard_map/while
  352.4 3.2 copy-start.1
  352.5 7.3 %copy-start.3 = (bf16[9,32]{1,0:T(8,128)(2,1)S(1)}, bf16[9,32]{1,0:T(8,128)(2,1)}, u32[]{:S(2)}) copy-start(bf16[9,32]{1,0:T(8,128)(2,1)} %get-tuple-element.413) | copy-start | bytes 1732 | tf_op jit(solution)/shard_map/while
Sparse Core Ops, SparseCore 0:
  56.6 54.2 all-gather.1
where the time goes:
time: 404 us; the launch traced here: 401 us
  matrix products  127 us (31%)
  waiting for transfers between devices  88.2 us (22%)
  other arithmetic  78.1 us (19%)
  local copies, waits for them, and re-layouts  56.3 us (14%)
  starting transfers between devices  29.3 us (7%)
  between operations  13.6 us (3%)
  loops' own time  8.92 us (2%)
    dot_general x36, matrix products, layer_two(): jnp.einsum('c,chw->hw', w_second[3 * row_shift + col_shift], padded[:, ro...  120 us
    convert_element_type x6, other arithmetic, layer_one(): return jnp.maximum(summed, 0.0).astype(jnp.bfloat16)  58.4 us
    all_gather x1, waiting for transfers between devices, shards(): lax.all_gather(owned, 'qry', axis=1, tiled=True)  53.4 us
    all_to_all x1, waiting for transfers between devices, shards(): lax.all_to_all(outgoing, 'ref', split_axis=0, concat_axis=0, tiled=True)  30 us
    mul x44, local copies, waits for them, and re-layouts, layer_one(): w_first[3 * row_shift + col_shift][:, None, None]  24.6 us
    all_to_all x1, starting transfers between devices, shards(): lax.all_to_all(outgoing, 'ref', split_axis=0, concat_axis=0, tiled=True)  14.8 us
    while x20, local copies, waits for them, and re-layouts  12.8 us
    scatter x8, other arithmetic, one_block(): hidden = hidden.at[:, :, :, 0].set(first).at[:, :, :, -1].set(final)  10.9 us
  transfers between devices with their start and end apart: 6, of which 3 were waited for; matrix products, arithmetic and copies ran while one was open for 1% of the time, Pallas kernels for 0%

commit v1 on v0

--- a/solution.py
+++ b/solution.py
@@ -5,6 +5,31 @@
 from jax.sharding import PartitionSpec as P
 
 FRAMES = 256
+
+
+def joined_along(blocks, dim):
+    shape = list(blocks.shape[1:])
+    shape[dim] *= blocks.shape[0]
+    return jnp.moveaxis(blocks, 0, dim).reshape(shape)
+
+
+def on_each_block(array, axis, dim, apply, out_dim):
+    devices, position, rows = (lax.axis_size(axis), lax.axis_index(axis), array.shape[dim])
+    upward = [(i, (i + 1) % devices) for i in range(devices)]
+    downward = [(i, (i - 1) % devices) for i in range(devices)]
+    half = devices // 2
+    blocks = {}
+    from_left = from_right = array
+    for lap in range(half + 1):
+        next_left = lax.ppermute(from_left, axis, upward) if lap < half else None
+        next_right = lax.ppermute(from_right, axis, downward) if lap < devices - half - 1 else None
+        blocks[-lap] = apply(from_left, (position - lap) % devices * rows)
+        if 0 < lap < devices - half:
+            blocks[lap] = apply(from_right, (position + lap) % devices * rows)
+        from_left, from_right = (next_left, next_right)
+    blocks = jnp.stack([blocks[k] for k in sorted(blocks)])
+    blocks = blocks[(jnp.arange(devices) - position + half) % devices]
+    return joined_along(blocks, out_dim)
 
 
 def with_halo(cells, sides, width):
@@ -89,11 +114,14 @@
     owned = jnp.einsum(
         "tsk,skrd->trd", placement, incoming, preferred_element_type=jnp.float32
     ).astype(jnp.bfloat16)
-    tiles = jnp.einsum(
-        "qd,brd->qbr",
-        queries,
-        lax.all_gather(owned, "qry", axis=1, tiled=True),
-        preferred_element_type=jnp.float32,
+    tiles = on_each_block(
+        owned,
+        "qry",
+        1,
+        lambda own_block, offset: jnp.einsum(
+            "qd,brd->qbr", queries, own_block, preferred_element_type=jnp.float32
+        ),
+        2,
     ).astype(jnp.bfloat16)
     panel_len = tiles.shape[2]
     ref_cols = blocks_dev * panel_len

time: 404 us -> 417 us (1.032)
  the two profiles are of different devices: /device:TPU:97 before, /device:TPU:1 now
where the time goes in v1:
time: 417 us; the launch traced here: 414 us
  matrix products  127 us (30%)
  starting transfers between devices  98.4 us (24%)
  other arithmetic  73.6 us (18%)
  local copies, waits for them, and re-layouts  60.7 us (15%)
  waiting for transfers between devices  45.8 us (11%)
  loops' own time  8.34 us (2%)
    dot_general x36, matrix products, layer_two(): jnp.einsum('c,chw->hw', w_second[3 * row_shift + col_shift], padded[:, ro...  120 us
    convert_element_type x6, other arithmetic, layer_one(): return jnp.maximum(summed, 0.0).astype(jnp.bfloat16)  58.4 us
    ppermute x7, starting transfers between devices, on_each_block(): lax.ppermute(from_right, axis, downward)  46.8 us
    all_to_all x1, waiting for transfers between devices, shards(): lax.all_to_all(outgoing, 'ref', split_axis=0, concat_axis=0, tiled=True)  33.5 us
    mul x44, local copies, waits for them, and re-layouts, layer_one(): w_first[3 * row_shift + col_shift][:, None, None]  24.6 us
    all_to_all x1, starting transfers between devices, shards(): lax.all_to_all(outgoing, 'ref', split_axis=0, concat_axis=0, tiled=True)  16.8 us
    ppermute x8, starting transfers between devices, on_each_block(): next_left = lax.ppermute(from_left, axis, upward) if lap < half else None  16.6 us
    ppermute x2, starting transfers between devices, with_halo(): lax.ppermute(tail, axis, [(i, (i + 1) % count) for i in range(ends)])  14.5 us
  transfers between devices with their start and end apart: 20, of which 9 were waited for; matrix products, arithmetic and copies ran while one was open for 2% of the time, Pallas kernels for 0%

profile of v1, /device:TPU:1, one launch (start us, length us, event | category | flops | bytes accessed | tf_op | source)
XLA Modules:
  0.0 414.0 jit_solution(568444930445860948)
XLA Ops:
  3.8 16.8 %all-to-all-start = ((bf16[32,1,8,1024]{3,2,1,0:T(8,128)(2,1)}), bf16[32,1,8,1024]{3,2,1,0:T(8,128)(2,1)S(1)}, u32[]{:S(2)}, u32[]{:S(2)}) async-start(bf16[32,1,8,1024]{3,2,1,0:T(8,128)(2,1)} %copy.147), calls=%async_computation | async-start | bytes 1048576 | tf_op jit(solution)/shard_map/all_to_all | solution.py:107
  20.6 33.5 %all-to-all-done = bf16[32,1,8,1024]{3,2,1,0:T(8,128)(2,1)S(1)} async-done(((bf16[32,1,8,1024]{3,2,1,0:T(8,128)(2,1)}), bf16[32,1,8,1024]{3,2,1,0:T(8,128)(2,1)S(1)}, u32[]{:S(2)}, u32[]{:S(2)}) %all-to-all-start) | async-done | bytes 524320 | tf_op jit(solution)/shard_map/all_to_all | solution.py:107
  54.7 3.2 collective-permute-start
  57.9 6.9 %collective-permute-done = bf16[8,8,1024]{2,0,1:T(8,128)(2,1)S(1)} collective-permute-done((bf16[8,8,1024]{2,0,1:T(8,128)(2,1)S(1)}, bf16[8,8,1024]{2,0,1:T(8,128)(2,1)S(1)}, u32[]{:S(2)}, u32[]{:S(2)}) %collective-permute-start) | collective-permute-done | bytes 131104 | tf_op jit(solution)/shard_map/ppermute | solution.py:24
  66.8 6.7 %collective-permute-start.8 = (bf16[8,8,1024]{2,0,1:T(8,128)(2,1)S(1)}, bf16[8,8,1024]{2,0,1:T(8,128)(2,1)S(1)}, u32[]{:S(2)}, u32[]{:S(2)}) collective-permute-start(bf16[8,8,1024]{2,0,1:T(8,128)(2,1)S(1)} %convolution_convert_fusion.1), channel_id=1, source_target_pairs={{0,15},{1,0},{2,1},{3,2},{4,3},{5,4},{6,5},{7,6},{8,7},{9,8},{10,9... | collective-permute-start | bytes 393224 | tf_op jit(solution)/shard_map/ppermute | solution.py:25
  75.8 6.7 %collective-permute-start.9 = (bf16[8,8,1024]{2,0,1:T(8,128)(2,1)S(1)}, bf16[8,8,1024]{2,0,1:T(8,128)(2,1)S(1)}, u32[]{:S(2)}, u32[]{:S(2)}) collective-permute-start(bf16[8,8,1024]{2,0,1:T(8,128)(2,1)S(1)} %collective-permute-done.8), channel_id=1, source_target_pairs={{0,15},{1,0},{2,1},{3,2},{4,3},{5,4},{6,5},{7,6},{8,7},{9,8},{10,9... | collective-permute-start | bytes 393224 | tf_op jit(solution)/shard_map/ppermute | solution.py:25
  84.8 6.7 %collective-permute-start.10 = (bf16[8,8,1024]{2,0,1:T(8,128)(2,1)S(1)}, bf16[8,8,1024]{2,0,1:T(8,128)(2,1)S(1)}, u32[]{:S(2)}, u32[]{:S(2)}) collective-permute-start(bf16[8,8,1024]{2,0,1:T(8,128)(2,1)S(1)} %collective-permute-done.9), channel_id=1, source_target_pairs={{0,15},{1,0},{2,1},{3,2},{4,3},{5,4},{6,5},{7,6},{8,7},{9,8},{10,9... | collective-permute-start | bytes 393224 | tf_op jit(solution)/shard_map/ppermute | solution.py:25
  93.8 6.7 %collective-permute-start.11 = (bf16[8,8,1024]{2,0,1:T(8,128)(2,1)S(1)}, bf16[8,8,1024]{2,0,1:T(8,128)(2,1)S(1)}, u32[]{:S(2)}, u32[]{:S(2)}) collective-permute-start(bf16[8,8,1024]{2,0,1:T(8,128)(2,1)S(1)} %collective-permute-done.10), channel_id=1, source_target_pairs={{0,15},{1,0},{2,1},{3,2},{4,3},{5,4},{6,5},{7,6},{8,7},{9,8},{10,9... | collective-permute-start | bytes 393224 | tf_op jit(solution)/shard_map/ppermute | solution.py:25
  102.9 6.7 %collective-permute-start.12 = (bf16[8,8,1024]{2,0,1:T(8,128)(2,1)S(1)}, bf16[8,8,1024]{2,0,1:T(8,128)(2,1)S(1)}, u32[]{:S(2)}, u32[]{:S(2)}) collective-permute-start(bf16[8,8,1024]{2,0,1:T(8,128)(2,1)S(1)} %collective-permute-done.11), channel_id=1, source_target_pairs={{0,15},{1,0},{2,1},{3,2},{4,3},{5,4},{6,5},{7,6},{8,7},{9,8},{10,9... | collective-permute-start | bytes 393224 | tf_op jit(solution)/shard_map/ppermute | solution.py:25
  111.9 6.7 %collective-permute-start.13 = (bf16[8,8,1024]{2,0,1:T(8,128)(2,1)S(1)}, bf16[8,8,1024]{2,0,1:T(8,128)(2,1)S(1)}, u32[]{:S(2)}, u32[]{:S(2)}) collective-permute-start(bf16[8,8,1024]{2,0,1:T(8,128)(2,1)S(1)} %collective-permute-done.12), channel_id=1, source_target_pairs={{0,15},{1,0},{2,1},{3,2},{4,3},{5,4},{6,5},{7,6},{8,7},{9,8},{10,9... | collective-permute-start | bytes 393224 | tf_op jit(solution)/shard_map/ppermute | solution.py:25
  122.4 6.7 %collective-permute-start.14 = (bf16[8,8,1024]{2,0,1:T(8,128)(2,1)S(1)}, bf16[8,8,1024]{2,0,1:T(8,128)(2,1)S(1)}, u32[]{:S(2)}, u32[]{:S(2)}) collective-permute-start(bf16[8,8,1024]{2,0,1:T(8,128)(2,1)S(1)} %collective-permute-done.13), channel_id=1, source_target_pairs={{0,15},{1,0},{2,1},{3,2},{4,3},{5,4},{6,5},{7,6},{8,7},{9,8},{10,9... | collective-permute-start | bytes 393224 | tf_op jit(solution)/shard_map/ppermute | solution.py:25
  134.6 10.8 %collective-permute-start.15 = (bf16[1,256,1]{1,2,0:T(2,128)(2,1)S(1)}, bf16[1,256,1]{1,2,0:T(2,128)(2,1)S(1)}, u32[]{:S(2)}, u32[]{:S(2)}) collective-permute-start(bf16[1,256,1]{1,2,0:T(2,128)(2,1)S(1)} %get-tuple-element.276), channel_id=1, source_target_pairs={{0,16},{16,32},{32,48},{48,64},{64,80},{80,96},{96,112},{112,128},... | collective-permute-start | bytes 1544 | tf_op jit(solution)/shard_map/ppermute | solution.py:43
  147.4 2.9 collective-permute-done.16
  153.9 3.6 collective-permute-start.17
  160.2 251.5 %while.15 = (s32[]{:T(128)}, bf16[4,1,256,256]{3,2,1,0:T(8,128)(2,1)}, f32[32]{0:T(128)}, f32[9,32]{1,0:T(8,128)S(1)}, s32[4]{0:T(128)}, /*index=5*/bf16[1,256,1...) while((s32[]{:T(128)}, ...), condition=%wide.region_3.4_spmd, body=%wide.region_2.3_spmd.sunk | while | flops 80692224 | bytes 89228328 | solution.py:156
  169.5 14.2 %maximum_convert_fusion.4 = bf16[1,32,256,258]{2,1,3,0:T(8,128)(2,1)S(1)} fusion(f32[256,258]{0,1:T(8,128)S(1)} %copy.238, f32[32]{0:T(128)S(1)} %get-tuple-element.395, f32[256,258]{0,1:T(8,128)} %copy.239, f32[32]{0:T(128)S(1)} %get-tuple-element.397, f32[256,258]{0,1:T(8,128)} %copy.240, f32[32]{0:T(128)S(1)} %get-tuple-element.399, ...), kind=kLoop, calls=%fused_computation.1.clone.1 | loop fusion | flops 42270720 | bytes 6606080 | tf_op jit(solution)/shard_map/while/body/eval_jaxpr/vmap()/convert_element_type | solution.py:64
  190.9 3.6 fusion.162
  194.6 3.6 fusion.163
  198.3 3.6 fusion.164
  202.0 2.8 fusion.165
  205.0 2.8 fusion.166
  211.0 3.6 fusion.168
  214.8 3.6 fusion.169
  218.5 3.6 fusion.170
  232.3 14.2 %maximum_convert_fusion.4 = bf16[1,32,256,258]{2,1,3,0:T(8,128)(2,1)S(1)} fusion(f32[256,258]{0,1:T(8,128)S(1)} %copy.238, f32[32]{0:T(128)S(1)} %get-tuple-element.395, f32[256,258]{0,1:T(8,128)} %copy.239, f32[32]{0:T(128)S(1)} %get-tuple-element.397, f32[256,258]{0,1:T(8,128)} %copy.240, f32[32]{0:T(128)S(1)} %get-tuple-element.399, ...), kind=kLoop, calls=%fused_computation.1.clone.1 | loop fusion | flops 42270720 | bytes 6606080 | tf_op jit(solution)/shard_map/while/body/eval_jaxpr/vmap()/convert_element_type | solution.py:64
  253.7 3.6 fusion.162
  257.5 3.6 fusion.163
  261.2 3.6 fusion.164
  264.9 2.8 fusion.165
  267.9 2.8 fusion.166
  273.9 3.6 fusion.168
  277.6 3.6 fusion.169
  281.4 3.6 fusion.170
  295.2 14.2 %maximum_convert_fusion.4 = bf16[1,32,256,258]{2,1,3,0:T(8,128)(2,1)S(1)} fusion(f32[256,258]{0,1:T(8,128)S(1)} %copy.238, f32[32]{0:T(128)S(1)} %get-tuple-element.395, f32[256,258]{0,1:T(8,128)} %copy.239, f32[32]{0:T(128)S(1)} %get-tuple-element.397, f32[256,258]{0,1:T(8,128)} %copy.240, f32[32]{0:T(128)S(1)} %get-tuple-element.399, ...), kind=kLoop, calls=%fused_computation.1.clone.1 | loop fusion | flops 42270720 | bytes 6606080 | tf_op jit(solution)/shard_map/while/body/eval_jaxpr/vmap()/convert_element_type | solution.py:64
  316.6 3.6 fusion.162
  320.3 3.6 fusion.163
  324.0 3.6 fusion.164
  330.8 2.8 fusion.166
  336.7 3.6 fusion.168
  340.5 3.6 fusion.169
  344.2 3.6 fusion.170
  358.1 14.2 %maximum_convert_fusion.4 = bf16[1,32,256,258]{2,1,3,0:T(8,128)(2,1)S(1)} fusion(f32[256,258]{0,1:T(8,128)S(1)} %copy.238, f32[32]{0:T(128)S(1)} %get-tuple-element.395, f32[256,258]{0,1:T(8,128)} %copy.239, f32[32]{0:T(128)S(1)} %get-tuple-element.397, f32[256,258]{0,1:T(8,128)} %copy.240, f32[32]{0:T(128)S(1)} %get-tuple-element.399, ...), kind=kLoop, calls=%fused_computation.1.clone.1 | loop fusion | flops 42270720 | bytes 6606080 | tf_op jit(solution)/shard_map/while/body/eval_jaxpr/vmap()/convert_element_type | solution.py:64
  379.5 3.6 fusion.162
  383.2 3.6 fusion.163
  386.9 3.6 fusion.164
  399.6 3.6 fusion.168
  403.4 3.6 fusion.169
  407.1 3.6 fusion.170
  (214 shorter events, 123.5 us)
Async XLA Ops:
  0.0 129.1 %copy-start = (bf16[256,1024]{1,0:T(8,128)(2,1)S(1)}, bf16[256,1024]{1,0:T(8,128)(2,1)}, u32[]{:S(2)}) copy-start(bf16[256,1024]{1,0:T(8,128)(2,1)} %param.13) | copy-start | bytes 1572868
  3.8 50.3 %all-to-all-start = ((bf16[32,1,8,1024]{3,2,1,0:T(8,128)(2,1)}), bf16[32,1,8,1024]{3,2,1,0:T(8,128)(2,1)S(1)}, u32[]{:S(2)}, u32[]{:S(2)}) async-start(bf16[32,1,8,1024]{3,2,1,0:T(8,128)(2,1)} %copy.147), calls=%async_computation | async-start | bytes 1048576 | tf_op jit(solution)/shard_map/all_to_all | solution.py:107
  54.7 10.1 %collective-permute-start = (bf16[8,8,1024]{2,0,1:T(8,128)(2,1)S(1)}, bf16[8,8,1024]{2,0,1:T(8,128)(2,1)S(1)}, u32[]{:S(2)}, u32[]{:S(2)}) collective-permute-start(bf16[8,8,1024]{2,0,1:T(8,128)(2,1)S(1)} %convolution_convert_fusion.1), channel_id=1, source_target_pairs={{0,1},{1,2},{2,3},{3,4},{4,5},{5,6},{6,7},{7,8},{8,9},{9,10},{10,1... | collective-permute-start | bytes 393224 | tf_op jit(solution)/shard_map/ppermute | solution.py:24
  64.8 9.0 %collective-permute-start.1 = (bf16[8,8,1024]{2,0,1:T(8,128)(2,1)S(1)}, bf16[8,8,1024]{2,0,1:T(8,128)(2,1)S(1)}, u32[]{:S(2)}, u32[]{:S(2)}) collective-permute-start(bf16[8,8,1024]{2,0,1:T(8,128)(2,1)S(1)} %collective-permute-done), channel_id=1, source_target_pairs={{0,1},{1,2},{2,3},{3,4},{4,5},{5,6},{6,7},{7,8},{8,9},{9,10},{10,1... | collective-permute-start | bytes 393224 | tf_op jit(solution)/shard_map/ppermute | solution.py:24
  66.8 9.0 %collective-permute-start.8 = (bf16[8,8,1024]{2,0,1:T(8,128)(2,1)S(1)}, bf16[8,8,1024]{2,0,1:T(8,128)(2,1)S(1)}, u32[]{:S(2)}, u32[]{:S(2)}) collective-permute-start(bf16[8,8,1024]{2,0,1:T(8,128)(2,1)S(1)} %convolution_convert_fusion.1), channel_id=1, source_target_pairs={{0,15},{1,0},{2,1},{3,2},{4,3},{5,4},{6,5},{7,6},{8,7},{9,8},{10,9... | collective-permute-start | bytes 393224 | tf_op jit(solution)/shard_map/ppermute | solution.py:25
  73.9 9.0 %collective-permute-start.2 = (bf16[8,8,1024]{2,0,1:T(8,128)(2,1)S(1)}, bf16[8,8,1024]{2,0,1:T(8,128)(2,1)S(1)}, u32[]{:S(2)}, u32[]{:S(2)}) collective-permute-start(bf16[8,8,1024]{2,0,1:T(8,128)(2,1)S(1)} %collective-permute-done.1), channel_id=1, source_target_pairs={{0,1},{1,2},{2,3},{3,4},{4,5},{5,6},{6,7},{7,8},{8,9},{9,10},{10,1... | collective-permute-start | bytes 393224 | tf_op jit(solution)/shard_map/ppermute | solution.py:24
  75.8 9.0 %collective-permute-start.9 = (bf16[8,8,1024]{2,0,1:T(8,128)(2,1)S(1)}, bf16[8,8,1024]{2,0,1:T(8,128)(2,1)S(1)}, u32[]{:S(2)}, u32[]{:S(2)}) collective-permute-start(bf16[8,8,1024]{2,0,1:T(8,128)(2,1)S(1)} %collective-permute-done.8), channel_id=1, source_target_pairs={{0,15},{1,0},{2,1},{3,2},{4,3},{5,4},{6,5},{7,6},{8,7},{9,8},{10,9... | collective-permute-start | bytes 393224 | tf_op jit(solution)/shard_map/ppermute | solution.py:25
  82.9 9.0 %collective-permute-start.3 = (bf16[8,8,1024]{2,0,1:T(8,128)(2,1)S(1)}, bf16[8,8,1024]{2,0,1:T(8,128)(2,1)S(1)}, u32[]{:S(2)}, u32[]{:S(2)}) collective-permute-start(bf16[8,8,1024]{2,0,1:T(8,128)(2,1)S(1)} %collective-permute-done.2), channel_id=1, source_target_pairs={{0,1},{1,2},{2,3},{3,4},{4,5},{5,6},{6,7},{7,8},{8,9},{9,10},{10,1... | collective-permute-start | bytes 393224 | tf_op jit(solution)/shard_map/ppermute | solution.py:24
  84.8 9.0 %collective-permute-start.10 = (bf16[8,8,1024]{2,0,1:T(8,128)(2,1)S(1)}, bf16[8,8,1024]{2,0,1:T(8,128)(2,1)S(1)}, u32[]{:S(2)}, u32[]{:S(2)}) collective-permute-start(bf16[8,8,1024]{2,0,1:T(8,128)(2,1)S(1)} %collective-permute-done.9), channel_id=1, source_target_pairs={{0,15},{1,0},{2,1},{3,2},{4,3},{5,4},{6,5},{7,6},{8,7},{9,8},{10,9... | collective-permute-start | bytes 393224 | tf_op jit(solution)/shard_map/ppermute | solution.py:25
  91.9 9.0 %collective-permute-start.4 = (bf16[8,8,1024]{2,0,1:T(8,128)(2,1)S(1)}, bf16[8,8,1024]{2,0,1:T(8,128)(2,1)S(1)}, u32[]{:S(2)}, u32[]{:S(2)}) collective-permute-start(bf16[8,8,1024]{2,0,1:T(8,128)(2,1)S(1)} %collective-permute-done.3), channel_id=1, source_target_pairs={{0,1},{1,2},{2,3},{3,4},{4,5},{5,6},{6,7},{7,8},{8,9},{9,10},{10,1... | collective-permute-start | bytes 393224 | tf_op jit(solution)/shard_map/ppermute | solution.py:24
  93.8 9.0 %collective-permute-start.11 = (bf16[8,8,1024]{2,0,1:T(8,128)(2,1)S(1)}, bf16[8,8,1024]{2,0,1:T(8,128)(2,1)S(1)}, u32[]{:S(2)}, u32[]{:S(2)}) collective-permute-start(bf16[8,8,1024]{2,0,1:T(8,128)(2,1)S(1)} %collective-permute-done.10), channel_id=1, source_target_pairs={{0,15},{1,0},{2,1},{3,2},{4,3},{5,4},{6,5},{7,6},{8,7},{9,8},{10,9... | collective-permute-start | bytes 393224 | tf_op jit(solution)/shard_map/ppermute | solution.py:25
  100.9 9.0 %collective-permute-start.5 = (bf16[8,8,1024]{2,0,1:T(8,128)(2,1)S(1)}, bf16[8,8,1024]{2,0,1:T(8,128)(2,1)S(1)}, u32[]{:S(2)}, u32[]{:S(2)}) collective-permute-start(bf16[8,8,1024]{2,0,1:T(8,128)(2,1)S(1)} %collective-permute-done.4), channel_id=1, source_target_pairs={{0,1},{1,2},{2,3},{3,4},{4,5},{5,6},{6,7},{7,8},{8,9},{9,10},{10,1... | collective-permute-start | bytes 393224 | tf_op jit(solution)/shard_map/ppermute | solution.py:24
  102.9 9.0 %collective-permute-start.12 = (bf16[8,8,1024]{2,0,1:T(8,128)(2,1)S(1)}, bf16[8,8,1024]{2,0,1:T(8,128)(2,1)S(1)}, u32[]{:S(2)}, u32[]{:S(2)}) collective-permute-start(bf16[8,8,1024]{2,0,1:T(8,128)(2,1)S(1)} %collective-permute-done.11), channel_id=1, source_target_pairs={{0,15},{1,0},{2,1},{3,2},{4,3},{5,4},{6,5},{7,6},{8,7},{9,8},{10,9... | collective-permute-start | bytes 393224 | tf_op jit(solution)/shard_map/ppermute | solution.py:25
  110.0 9.0 %collective-permute-start.6 = (bf16[8,8,1024]{2,0,1:T(8,128)(2,1)S(1)}, bf16[8,8,1024]{2,0,1:T(8,128)(2,1)S(1)}, u32[]{:S(2)}, u32[]{:S(2)}) collective-permute-start(bf16[8,8,1024]{2,0,1:T(8,128)(2,1)S(1)} %collective-permute-done.5), channel_id=1, source_target_pairs={{0,1},{1,2},{2,3},{3,4},{4,5},{5,6},{6,7},{7,8},{8,9},{9,10},{10,1... | collective-permute-start | bytes 393224 | tf_op jit(solution)/shard_map/ppermute | solution.py:24
  111.9 10.5 %collective-permute-start.13 = (bf16[8,8,1024]{2,0,1:T(8,128)(2,1)S(1)}, bf16[8,8,1024]{2,0,1:T(8,128)(2,1)S(1)}, u32[]{:S(2)}, u32[]{:S(2)}) collective-permute-start(bf16[8,8,1024]{2,0,1:T(8,128)(2,1)S(1)} %collective-permute-done.12), channel_id=1, source_target_pairs={{0,15},{1,0},{2,1},{3,2},{4,3},{5,4},{6,5},{7,6},{8,7},{9,8},{10,9... | collective-permute-start | bytes 393224 | tf_op jit(solution)/shard_map/ppermute | solution.py:25
  119.0 10.1 %collective-permute-start.7 = (bf16[8,8,1024]{2,0,1:T(8,128)(2,1)S(1)}, bf16[8,8,1024]{2,0,1:T(8,128)(2,1)S(1)}, u32[]{:S(2)}, u32[]{:S(2)}) collective-permute-start(bf16[8,8,1024]{2,0,1:T(8,128)(2,1)S(1)} %collective-permute-done.6), channel_id=1, source_target_pairs={{0,1},{1,2},{2,3},{3,4},{4,5},{5,6},{6,7},{7,8},{8,9},{9,10},{10,1... | collective-permute-start | bytes 393224 | tf_op jit(solution)/shard_map/ppermute | solution.py:24
  122.4 11.1 %collective-permute-start.14 = (bf16[8,8,1024]{2,0,1:T(8,128)(2,1)S(1)}, bf16[8,8,1024]{2,0,1:T(8,128)(2,1)S(1)}, u32[]{:S(2)}, u32[]{:S(2)}) collective-permute-start(bf16[8,8,1024]{2,0,1:T(8,128)(2,1)S(1)} %collective-permute-done.13), channel_id=1, source_target_pairs={{0,15},{1,0},{2,1},{3,2},{4,3},{5,4},{6,5},{7,6},{8,7},{9,8},{10,9... | collective-permute-start | bytes 393224 | tf_op jit(solution)/shard_map/ppermute | solution.py:25
  133.8 13.6 %copy-start.2 = (f32[9,32]{1,0:T(8,128)S(1)}, f32[9,32]{1,0:T(8,128)}, u32[]{:S(2)}) copy-start(f32[9,32]{1,0:T(8,128)} %param.17) | copy-start | bytes 3460
  134.6 12.8 %collective-permute-start.15 = (bf16[1,256,1]{1,2,0:T(2,128)(2,1)S(1)}, bf16[1,256,1]{1,2,0:T(2,128)(2,1)S(1)}, u32[]{:S(2)}, u32[]{:S(2)}) collective-permute-start(bf16[1,256,1]{1,2,0:T(2,128)(2,1)S(1)} %get-tuple-element.276), channel_id=1, source_target_pairs={{0,16},{16,32},{32,48},{48,64},{64,80},{80,96},{96,112},{112,128},... | collective-permute-start | bytes 1544 | tf_op jit(solution)/shard_map/ppermute | solution.py:43
  145.4 4.9 %collective-permute-start.16 = (bf16[1,256,1]{1,2,0:T(2,128)(2,1)S(1)}, bf16[1,256,1]{1,2,0:T(2,128)(2,1)S(1)}, u32[]{:S(2)}, u32[]{:S(2)}) collective-permute-start(bf16[1,256,1]{1,2,0:T(2,128)(2,1)S(1)} %get-tuple-element.275), channel_id=1, source_target_pairs={{16,0},{32,16},{48,32},{64,48},{80,64},{96,80},{112,96},{128,112},... | collective-permute-start | bytes 1544 | tf_op jit(solution)/shard_map/ppermute | solution.py:45
  151.2 8.4 %collective-permute-start.18 = (bf16[1,1,32,256]{3,2,1,0:T(8,128)(2,1)S(1)}, bf16[1,1,32,256]{3,2,1,0:T(8,128)(2,1)}, u32[]{:S(2)}, u32[]{:S(2)}) collective-permute-start(bf16[1,1,32,256]{3,2,1,0:T(8,128)(2,1)S(1)} %maximum_convert_fusion.1), channel_id=1, source_target_pairs={{16,0},{32,16},{48,32},{64,48},{80,64},{96,80},{112,96},{128,112},... | collective-permute-start | bytes 49160 | tf_op jit(solution)/shard_map/ppermute | solution.py:45
  153.9 5.7 %collective-permute-start.17 = (bf16[1,1,32,256]{3,2,1,0:T(8,128)(2,1)S(1)}, bf16[1,1,32,256]{3,2,1,0:T(8,128)(2,1)}, u32[]{:S(2)}, u32[]{:S(2)}) collective-permute-start(bf16[1,1,32,256]{3,2,1,0:T(8,128)(2,1)S(1)} %maximum_convert_fusion.2), channel_id=1, source_target_pairs={{0,16},{16,32},{32,48},{48,64},{64,80},{80,96},{96,112},{112,128},... | collective-permute-start | bytes 49160 | tf_op jit(solution)/shard_map/ppermute | solution.py:43
  183.7 3.2 copy-start.1
  183.7 7.2 %copy-start.3 = (bf16[9,32]{1,0:T(8,128)(2,1)S(1)}, bf16[9,32]{1,0:T(8,128)(2,1)}, u32[]{:S(2)}) copy-start(bf16[9,32]{1,0:T(8,128)(2,1)} %get-tuple-element.453) | copy-start | bytes 1732 | tf_op jit(solution)/shard_map/while
  246.6 3.2 copy-start.1
  246.6 7.2 %copy-start.3 = (bf16[9,32]{1,0:T(8,128)(2,1)S(1)}, bf16[9,32]{1,0:T(8,128)(2,1)}, u32[]{:S(2)}) copy-start(bf16[9,32]{1,0:T(8,128)(2,1)} %get-tuple-element.453) | copy-start | bytes 1732 | tf_op jit(solution)/shard_map/while
  309.4 3.2 copy-start.1
  309.5 7.2 %copy-start.3 = (bf16[9,32]{1,0:T(8,128)(2,1)S(1)}, bf16[9,32]{1,0:T(8,128)(2,1)}, u32[]{:S(2)}) copy-start(bf16[9,32]{1,0:T(8,128)(2,1)} %get-tuple-element.453) | copy-start | bytes 1732 | tf_op jit(solution)/shard_map/while
  372.3 3.2 copy-start.1
  372.3 7.2 %copy-start.3 = (bf16[9,32]{1,0:T(8,128)(2,1)S(1)}, bf16[9,32]{1,0:T(8,128)(2,1)}, u32[]{:S(2)}) copy-start(bf16[9,32]{1,0:T(8,128)(2,1)} %get-tuple-element.453) | copy-start | bytes 1732 | tf_op jit(solution)/shard_map/while
